TPU v7x, 32 devices: a whole 2x2x4 slice. The times are simulated.
32 devices in a mesh: prow: 16 (over z, y, core), pcol: 2 (over x).
Axes of the slice: x: 2, y: 2, z: 4, core: 2. Of those that a mesh axis runs over, the one named last changes fastest.
Arguments:
- inverse: float32 [2048, 2048], P('prow', 'pcol'), may hold values from -12 to 12, as said below
- factor_one: bfloat16 [2048, 512], P('prow'), may hold values from -0.1875 to 0.1875
- factor_two: bfloat16 [2048, 512], P('prow'), may hold values from -0.1875 to 0.1875
- factor_top: bfloat16 [512, 512], replicated, may hold values from -0.1875 to 0.1875
- diag_one: float32 [512, 512], replicated, may hold values from -2 to 4, as said below
- diag_two: float32 [512, 512], replicated, may hold values from -2 to 4, as said below
- pattern: int32 [2, 8], replicated, may hold values from 0 to 15, as said below
Outputs:
- inv_cols_one: float32 [2048, 512], P(('prow', 'pcol'))
- diag_block_one: float32 [512, 512], replicated
- inv_cols_two: float32 [2048, 512], P(('prow', 'pcol'))
- inv_top_two: float32 [512, 512], replicated
- diag_block_two: float32 [512, 512], replicated
Inputs may be any that keep to these rules, and one draw needn't show every extreme that they name: `pattern`: each row lists 8 distinct ancestor blocks in rising order; blocks 0 and 8 are in both rows. `inverse`: Symmetric. `diag_one`: Symmetric. `diag_two`: Symmetric.
All inputs are finite; a program needn't handle non-finite values.
Results may differ from a plain program's by a relative error of at most 0.0003.
Values may be sent and summed in bfloat16 or wider, within the bound.
A program may use at most 64 MiB of HBM per device.

v0:
```python
import jax
import jax.numpy as jnp
from jax import lax
from jax.sharding import PartitionSpec as P

BLOCK = 128
highest_precision = lax.Precision.HIGHEST


def broadcast(x, axis, root):
    mine = lax.axis_index(axis) == root
    return lax.psum(jnp.where(mine, x, jnp.zeros_like(x)), axis)


def product(left, right):
    return jnp.dot(left, right, precision=highest_precision, preferred_element_type=jnp.float32)


def row_mask(pattern_row, leading_row_index, row_count):
    row_ids = leading_row_index + lax.iota(jnp.int32, row_count)
    hits = (row_ids // BLOCK)[:, None] == pattern_row[None, :]
    return jnp.max(hits.astype(jnp.float32), axis=1)


def masked(columns, column_mask):
    return columns * column_mask[:, None].astype(jnp.bfloat16)


def multiply(inverse, columns):
    return product(inverse, columns)


def fetch_columns(factor_local, group_ratio, column_group):
    pieces = []
    for offset in range(group_ratio):
        pieces.append(broadcast(factor_local, "prow", group_ratio * column_group + offset))
    return jnp.concatenate(pieces, axis=0)


def reduce_rows(inverse, columns):
    return lax.psum_scatter(multiply(inverse, columns), "pcol", scatter_dimension=0, tiled=True)


def block_sums(inv_cols_one, own_one, own_two):
    correction = product(own_one.T, inv_cols_one)
    mirrored = product(inv_cols_one.T, own_two)
    return lax.psum((correction, mirrored), ("prow", "pcol"))


def shards(inverse, factor_one, factor_two, factor_top, diag_one, diag_two, pattern):
    row_count = inverse.shape[0]
    column_count = inverse.shape[1]
    pcol_size = lax.axis_size("pcol")
    group_ratio = lax.axis_size("prow") // pcol_size
    row_group = lax.axis_index("prow")
    column_group = lax.axis_index("pcol")
    keep_rows = row_count // pcol_size
    row_first = row_group * row_count
    column_first = column_group * column_count
    own_local = column_group * keep_rows
    own_first = row_first + own_local
    own_mask_one = row_mask(pattern[0], own_first, keep_rows)
    own_mask_two = row_mask(pattern[1], own_first, keep_rows)
    own_one = (
        lax.dynamic_slice_in_dim(factor_one, own_local, keep_rows, 0).astype(jnp.float32)
        * own_mask_one[:, None]
    )
    own_two = (
        lax.dynamic_slice_in_dim(factor_two, own_local, keep_rows, 0).astype(jnp.float32)
        * own_mask_two[:, None]
    )
    column_mask_one = row_mask(pattern[0], column_first, column_count)
    column_mask_two = row_mask(pattern[1], column_first, column_count)
    columns_one = masked(fetch_columns(factor_one, group_ratio, column_group), column_mask_one)
    share_one = reduce_rows(inverse, columns_one)
    inv_cols_one = -(own_mask_one[:, None] * share_one)
    correction_one, mirrored = block_sums(inv_cols_one, own_one, own_two)
    columns_two = masked(fetch_columns(factor_two, group_ratio, column_group), column_mask_two)
    share_two = reduce_rows(inverse, columns_two)
    diag_block_one = diag_one - correction_one
    inv_cols_two = -(own_mask_two[:, None] * (share_two + product(inv_cols_one, factor_top)))
    inv_top_two = -(mirrored + product(diag_block_one, factor_top))
    correction_two = lax.psum(product(own_two.T, inv_cols_two), ("prow", "pcol"))
    diag_block_two = diag_two - correction_two - product(factor_top.T, inv_top_two)
    return (inv_cols_one, diag_block_one, inv_cols_two, inv_top_two, diag_block_two)


def solution(mesh):
    in_specs = (P("prow", "pcol"), P("prow", None), P("prow", None), P(), P(), P(), P())
    out_specs = (P(("prow", "pcol"), None), P(), P(("prow", "pcol"), None), P(), P())
    return jax.shard_map(shards, mesh=mesh, in_specs=in_specs, out_specs=out_specs, check_vma=False)
```

profile of v0, /device:TPU:0, one launch (start us, length us, event | category | flops | bytes accessed | tf_op | source)
XLA Modules:
  0.0 309.8 jit_solution(8373516454459245324)
XLA Ops:
  7.2 2.3 broadcast_select_fusion
  9.7 0.8 copy-done.10
  11.5 107.1 %all-reduce.7.cloned.1.call-done = (bf16[128,512]{1,0:T(8,128)(2,1)}, bf16[128,512]{1,0:T(8,128)(2,1)}, bf16[128,512]{1,0:T(8,128)(2,1)}, bf16[128,512]{1,0:T(8,...) async-done(((bf16[128,512]{1,0:T(8,128)(2,1)}, ...) | async-done | bytes 2097168 | tf_op jit(solution)/shard_map/psum | solution.py:12
  118.6 0.9 constant_dynamic-update-slice_fusion.7
  119.6 0.9 copy-done.24
  120.5 0.9 copy-done.23
  121.5 0.8 copy-done.21
  122.4 0.9 copy-done.19
  123.3 1.4 convolution_bitcast_fusion.2
  124.7 0.8 copy.27
  125.6 0.8 copy-done.18
  126.5 0.9 copy-done.17
  127.4 0.9 copy-done.16
  128.3 0.9 copy-done.15
  129.2 0.9 copy-done.14
  130.1 0.9 copy-done.13
  131.0 0.9 copy-done.12
  131.9 0.9 copy-done.11
  132.8 1.4 convolution_bitcast_fusion.1
  134.2 0.8 copy.29
  135.1 2.1 reduce-scatter.7.cloned.1.call-done
  137.2 1.0 copy.28
  138.3 0.9 copy-done.8
  139.2 2.0 fusion.12
  141.2 2.0 fusion.8
  143.2 8.6 %reduce-scatter.9.cloned.1.call-done = f32[64,512]{1,0:T(8,128)} async-done(((f32[128,512]{1,0:T(8,128)}), f32[64,512]{1,0:T(8,128)}) %reduce-scatter.9.cloned.1.call-update) | async-done | bytes 131088 | tf_op jit(solution)/shard_map/reduce_scatter | solution.py:41
  151.8 1.3 fusion.3
  153.1 2.1 fusion.11
  156.0 141.7 %all-reduce.5.cloned.1.call-done = (f32[512,512]{1,0:T(8,128)}, f32[512,512]{1,0:T(8,128)}, f32[512,512]{1,0:T(8,128)}) async-done(((f32[512,512]{1,0:T(8,128)}, f32[512,512]{1,0:T(8,128)}, f32[512,512]{1,0:T(8,128)}), (f32[512,512]{1,0:T(8,128)}, f32[512,512]{1,0:T(8,128)}, f32[512,512]{1,0:T(8,128)})) %all-reduce.5.cloned.1.call-update) | async-done | bytes 3145744 | tf_op jit(solution)/shard_map/psum | solution.py:47
  297.7 1.5 sub.27
  299.2 1.0 fusion
  301.1 2.1 fusion.1
  (72 shorter events, 3.2 us)
Async XLA Ops:
  7.2 144.6 %copy-start = (bf16[512,512]{1,0:T(8,128)(2,1)S(1)}, bf16[512,512]{1,0:T(8,128)(2,1)}, u32[]{:S(2)}) copy-start(bf16[512,512]{1,0:T(8,128)(2,1)} %param.10) | copy-start | bytes 1572868
  7.2 111.4 %all-reduce.7.cloned.1.call-start = ((), (), s32[]{:S(2)}) async-start(), calls=%async_computation.5 | async-start | bytes 4194304 | tf_op jit(solution)/shard_map/psum | solution.py:12
  9.6 0.9 copy-start.10
  9.6 127.6 %reduce-scatter.7.cloned.1.call-start = ((), (), s32[]{:S(2)}) async-start(), calls=%async_computation.2 | async-start | bytes 393216
  10.6 0.7 copy-start.26
  118.6 1.0 copy-start.25
  119.6 0.9 copy-start.24
  120.5 0.9 copy-start.23
  120.5 1.0 copy-start.22
  121.4 0.9 copy-start.21
  121.4 1.0 copy-start.20
  121.5 1.8 copy-start.3
  122.4 0.9 copy-start.19
  125.6 0.9 copy-start.18
  125.6 26.2 %reduce-scatter.9.cloned.1.call-start = ((), (), s32[]{:S(2)}) async-start(), calls=%async_computation.3 | async-start | bytes 393216 | tf_op jit(solution)/shard_map/reduce_scatter | solution.py:41
  126.5 0.9 copy-start.17
  127.4 0.9 copy-start.16
  128.3 0.9 copy-start.15
  129.2 0.9 copy-start.14
  130.1 0.9 copy-start.13
  131.0 0.9 copy-start.12
  131.9 0.9 copy-start.11
  135.1 162.6 %all-reduce.5.cloned.1.call-start = ((), (), s32[]{:S(2)}) async-start(), calls=%async_computation.4 | async-start | bytes 6291456 | tf_op jit(solution)/shard_map/psum | solution.py:47
  138.3 0.9 copy-start.8
  153.1 2.1 copy-start.9
  155.2 142.5 %copy-start.4 = (f32[512,512]{1,0:T(8,128)S(1)}, f32[512,512]{1,0:T(8,128)}, u32[]{:S(2)}) copy-start(f32[512,512]{1,0:T(8,128)} %param.11) | copy-start | bytes 3145732
  297.7 1.5 copy-start.5
  299.2 1.0 copy-start.1
  299.2 1.6 copy-start.6
  299.2 1.9 copy-start.7
  300.3 3.0 copy-start.2
Sparse Core Ops, SparseCore 0:
  14.0 104.6 all-reduce.6
  125.7 11.4 reduce-scatter.6
  140.0 11.6 reduce-scatter.8
  159.0 138.6 all-reduce.4
where the time goes:
time: 310 us
  waiting for transfers between devices  260 us (84%)
  local copies, waits for them, and re-layouts  18.6 us (6%)
  between operations  14 us (5%)
  matrix products  13.3 us (4%)
  other arithmetic  4.09 us (1%)
    psum x1, waiting for transfers between devices, block_sums(): return lax.psum((correction, mirrored), ('prow', 'pcol'))  142 us
    psum x1, waiting for transfers between devices, broadcast(): return lax.psum(jnp.where(mine, x, jnp.zeros_like(x)), axis)  107 us
    unnamed x73, local copies, waits for them, and re-layouts  18.6 us
    dot_general x8, matrix products, product(): jnp.dot(left, right, precision=highest_precision, preferred_element_type=...  13.3 us
    reduce_scatter x1, waiting for transfers between devices, reduce_rows(): lax.psum_scatter(multiply(inverse, columns), 'pcol', scatter_dimension=0,...  8.6 us
  transfers between devices with their start and end apart: 4, of which 4 were waited for; matrix products, arithmetic and copies ran while one was open for 3% of the time, Pallas kernels for 0%

commit v1 on v0

--- a/solution.py
+++ b/solution.py
@@ -44,7 +44,13 @@
 def block_sums(inv_cols_one, own_one, own_two):
     correction = product(own_one.T, inv_cols_one)
     mirrored = product(inv_cols_one.T, own_two)
-    return lax.psum((correction, mirrored), ("prow", "pcol"))
+
+    def _pack_ends(message):
+        for num in ("pcol", "prow"):
+            message = lax.psum(message, num)
+        return message
+
+    return _pack_ends((correction, mirrored))
 
 
 def shards(inverse, factor_one, factor_two, factor_top, diag_one, diag_two, pattern):

time: 310 us -> 468 us (1.51)
  waiting for transfers between devices: 260 us -> 417 us
    psum x1 -> x3, waiting for transfers between devices: 142 us -> 284 us  [the longest x2 151 us: _pack_ends(): message = lax.psum(message, num)]
    unnamed x5 -> x7, waiting for transfers between devices: 2.18 us -> 10.6 us
    reduce_scatter x1, waiting for transfers between devices: 8.6 us -> 14.4 us  [reduce_rows(): lax.psum_scatter(multiply(inverse, columns), 'pcol', scatter_dimension=0,...]
    unnamed x73 -> x69, local copies, waits for them, and re-layouts: 18.6 us -> 16.9 us
  transfers between devices with their start and end apart: 4 -> 6, of which waited for: 4 -> 6; matrix products, arithmetic and copies ran while one was open for 3% -> 2% of each run, Pallas kernels for 0% -> 0%
where the time goes in v1:
time: 468 us
  waiting for transfers between devices  417 us (89%)
  local copies, waits for them, and re-layouts  17 us (4%)
  matrix products  14.7 us (3%)
  between operations  14.4 us (3%)
    psum x2, waiting for transfers between devices, _pack_ends(): message = lax.psum(message, num)  151 us
    psum x1, waiting for transfers between devices, shards(): lax.psum(product(own_two.T, inv_cols_two), ('prow', 'pcol'))  133 us
    psum x1, waiting for transfers between devices, broadcast(): return lax.psum(jnp.where(mine, x, jnp.zeros_like(x)), axis)  108 us
    unnamed x69, local copies, waits for them, and re-layouts  16.9 us
    dot_general x8, matrix products, product(): jnp.dot(left, right, precision=highest_precision, preferred_element_type=...  14.7 us
    reduce_scatter x1, waiting for transfers between devices, reduce_rows(): lax.psum_scatter(multiply(inverse, columns), 'pcol', scatter_dimension=0,...  14.4 us
    unnamed x7, waiting for transfers between devices  10.6 us
  transfers between devices with their start and end apart: 6, of which 6 were waited for; matrix products, arithmetic and copies ran while one was open for 2% of the time, Pallas kernels for 0%

profile of v1, /device:TPU:0, one launch (start us, length us, event | category | flops | bytes accessed | tf_op | source)
XLA Modules:
  0.0 467.7 jit_solution(4237819168914070375)
XLA Ops:
  7.2 2.3 broadcast_select_fusion
  10.4 108.2 %all-reduce.14.cloned.1.call-done = (bf16[128,512]{1,0:T(8,128)(2,1)}, bf16[128,512]{1,0:T(8,128)(2,1)}, bf16[128,512]{1,0:T(8,128)(2,1)}, bf16[128,512]{1,0:T(8...) async-done(((bf16[128,512]{1,0:T(8,128)(2,1)}, ...) | async-done | bytes 2097168 | tf_op jit(solution)/shard_map/psum | solution.py:12
  118.6 0.9 constant_dynamic-update-slice_fusion.7
  119.6 0.9 copy-done.22
  120.5 0.9 copy-done.21
  121.5 0.8 copy-done.19
  122.4 0.9 copy-done.17
  123.3 1.4 convolution_bitcast_fusion.2
  124.7 0.8 copy.27
  126.7 10.5 %reduce-scatter.7.cloned.1.call-done = f32[64,512]{1,0:T(8,128)} async-done(((f32[128,512]{1,0:T(8,128)}), f32[64,512]{1,0:T(8,128)}) %reduce-scatter.7.cloned.1.call-update) | async-done | bytes 131088
  137.2 1.0 copy.28
  138.3 2.0 fusion.8
  140.3 2.0 fusion.12
  142.4 0.8 copy-done.16
  143.2 0.9 copy-done.15
  144.1 0.9 copy-done.14
  145.0 0.9 copy-done.13
  145.9 0.9 copy-done.12
  146.8 0.9 copy-done.11
  147.8 0.9 copy-done.10
  148.7 0.9 copy-done.9
  149.6 1.4 convolution_bitcast_fusion.1
  151.0 0.8 copy.29
  151.9 53.7 %all-reduce.12.cloned.1.call-done = (f32[512,512]{1,0:T(8,128)}, f32[512,512]{1,0:T(8,128)}) async-done(((f32[512,512]{1,0:T(8,128)}, f32[512,512]{1,0:T(8,128)}), (f32[512,512]{1,0:T(8,128)}, f32[512,512]{1,0:T(8,128)})) %all-reduce.12.cloned.1.call-update) | async-done | bytes 2097168 | tf_op jit(solution)/shard_map/psum | solution.py:50
  205.7 14.4 %reduce-scatter.9.cloned.1.call-done = f32[64,512]{1,0:T(8,128)} async-done(((f32[128,512]{1,0:T(8,128)}), f32[64,512]{1,0:T(8,128)}) %reduce-scatter.9.cloned.1.call-update) | async-done | bytes 131088 | tf_op jit(solution)/shard_map/reduce_scatter | solution.py:41
  220.0 1.3 fusion.3
  221.4 2.1 fusion.11
  224.2 97.2 %all-reduce.10.cloned.1.call-done = (f32[512,512]{1,0:T(8,128)}, f32[512,512]{1,0:T(8,128)}) async-done(((f32[512,512]{1,0:T(8,128)}, f32[512,512]{1,0:T(8,128)}), (f32[512,512]{1,0:T(8,128)}, f32[512,512]{1,0:T(8,128)})) %all-reduce.10.cloned.1.call-update) | async-done | bytes 2097168 | tf_op jit(solution)/shard_map/psum | solution.py:50
  321.5 1.5 sub.27
  323.0 1.0 fusion
  324.1 133.2 %all-reduce.8.cloned.1.call-done = f32[512,512]{1,0:T(8,128)} async-done(((f32[512,512]{1,0:T(8,128)}), f32[512,512]{1,0:T(8,128)}) %all-reduce.8.cloned.1.call-update) | async-done | bytes 1048592 | tf_op jit(solution)/shard_map/psum | solution.py:89
  457.2 3.6 fusion.1
  (74 shorter events, 3.3 us)
Async XLA Ops:
  7.2 212.9 %copy-start = (bf16[512,512]{1,0:T(8,128)(2,1)S(1)}, bf16[512,512]{1,0:T(8,128)(2,1)}, u32[]{:S(2)}) copy-start(bf16[512,512]{1,0:T(8,128)(2,1)} %param.10) | copy-start | bytes 1572868
  7.2 111.4 %all-reduce.14.cloned.1.call-start = ((), (), s32[]{:S(2)}) async-start(), calls=%async_computation.7 | async-start | bytes 4194304 | tf_op jit(solution)/shard_map/psum | solution.py:12
  9.6 127.6 %reduce-scatter.7.cloned.1.call-start = ((), (), s32[]{:S(2)}) async-start(), calls=%async_computation.3 | async-start | bytes 393216
  9.7 0.7 copy-start.24
  118.6 1.0 copy-start.23
  119.6 0.9 copy-start.22
  120.5 0.9 copy-start.21
  120.5 1.0 copy-start.20
  121.4 0.9 copy-start.19
  121.4 1.0 copy-start.18
  121.5 1.8 copy-start.3
  122.4 0.9 copy-start.17
  125.6 0.9 copy-start.8
  125.6 80.0 %all-reduce.12.cloned.1.call-start = ((), (), s32[]{:S(2)}) async-start(), calls=%async_computation.6 | async-start | bytes 4194304 | tf_op jit(solution)/shard_map/psum | solution.py:50
  138.3 2.0 copy-start.6
  142.3 0.9 copy-start.16
  142.3 77.7 %reduce-scatter.9.cloned.1.call-start = ((), (), s32[]{:S(2)}) async-start(), calls=%async_computation.4 | async-start | bytes 393216 | tf_op jit(solution)/shard_map/reduce_scatter | solution.py:41
  143.2 0.9 copy-start.15
  144.1 0.9 copy-start.14
  145.0 0.9 copy-start.13
  145.9 0.9 copy-start.12
  146.8 0.9 copy-start.11
  147.7 0.9 copy-start.10
  148.7 0.9 copy-start.9
  151.9 169.6 %all-reduce.10.cloned.1.call-start = ((), (), s32[]{:S(2)}) async-start(), calls=%async_computation.5 | async-start | bytes 4194304 | tf_op jit(solution)/shard_map/psum | solution.py:50
  205.6 251.6 %all-reduce.8.cloned.1.call-start = ((), (), s32[]{:S(2)}) async-start(), calls=%async_computation.2 | async-start | bytes 2097152 | tf_op jit(solution)/shard_map/psum | solution.py:89
  221.3 2.1 copy-start.7
  221.4 100.1 %copy-start.4 = (f32[512,512]{1,0:T(8,128)S(1)}, f32[512,512]{1,0:T(8,128)}, u32[]{:S(2)}) copy-start(f32[512,512]{1,0:T(8,128)} %param.11) | copy-start | bytes 3145732
  321.5 1.5 copy-start.5
  323.0 1.0 copy-start.1
  324.1 136.8 %copy-start.2 = (f32[512,512]{1,0:T(8,128)}, f32[512,512]{1,0:T(8,128)S(1)}, u32[]{:S(2)}) copy-start(f32[512,512]{1,0:T(8,128)S(1)} %fusion) | copy-start | bytes 3145732
Sparse Core Ops, SparseCore 0:
  14.0 104.6 all-reduce.13
  125.7 11.4 reduce-scatter.6
  142.4 63.1 all-reduce.11
  208.3 11.6 reduce-scatter.8
  223.5 97.9 all-reduce.9
  327.9 129.2 all-reduce.7
